TPU v7x, 512 devices: a whole 4x4x16 slice. The times are simulated.
512 devices in a mesh: prow: 32 (over x, y, core), pcol: 16 (over z).
Axes of the slice: x: 4, y: 4, z: 16, core: 2. Of those that a mesh axis runs over, the one named last changes fastest.
Arguments:
- slab: float32 [32768, 4096], P('prow', 'pcol'), may hold values from -6 to 6
- panel: float32 [32768, 256], P('prow', 'pcol'), may hold values from -0.1875 to 0.1875
- pivots: int32 [256], replicated, may hold values from 256 to 32767, as said below
Outputs:
- result: float32 [32768, 4096], P('prow', 'pcol')
Inputs may be any that keep to these rules, and one draw needn't show every extreme that they name: `pivots`: 256 distinct rows, none among the first 256; at most 32 of them lie in the 1024 rows of one process row, and some process row holds exactly 32.
All inputs are finite; a program needn't handle non-finite values.
Results may differ from a plain program's by a relative error of at most 0.00005.
Values sent between devices are 32-bit elements; how exact they have to be, the bound alone decides.
A program may use at most 64 MiB of HBM per device.

v0:
```python
import jax
import jax.numpy as jnp
from jax import lax
from jax.sharding import PartitionSpec as P


def broadcast(value, axis, root):
    mine = lax.axis_index(axis) == root
    return lax.psum(jnp.where(mine, value, jnp.zeros_like(value)), axis)


def solve_block(diag_block, right_side):
    return jax.scipy.linalg.solve_triangular(diag_block, right_side, lower=True, unit_diagonal=True)


def local(slab, panel, pivots):
    row_count = slab.shape[0]
    panel_width = pivots.shape[0]
    row_index = lax.axis_index("prow")
    row_start = row_index * row_count
    held_here = pivots // row_count == row_index
    local_row = jnp.clip(pivots - row_start, 0, row_count - 1)
    picked = jnp.take(slab, local_row, axis=0)
    masked = jnp.where(held_here[:, None], picked, jnp.zeros_like(picked))
    leading, diag_piece = (
        broadcast(slab[:panel_width], "prow", 0),
        broadcast(panel[:panel_width], "prow", 0),
    )
    diag_block = lax.all_gather(diag_piece, "pcol", axis=1, tiled=True)
    pivot_rows = lax.psum(masked, "prow")
    upper_rows = solve_block(diag_block, pivot_rows)
    target_row = jnp.where(held_here, local_row, row_count)
    swapped = slab.at[target_row].set(leading, mode="drop")
    updated = swapped - jnp.dot(
        lax.all_gather(panel, "pcol", axis=1, tiled=True),
        upper_rows,
        precision=lax.Precision.HIGHEST,
        preferred_element_type=jnp.float32,
    )
    top_block = jnp.where(row_index == 0, upper_rows, updated[:panel_width])
    return updated.at[:panel_width].set(top_block)


def solution(mesh):
    return jax.shard_map(
        local,
        mesh=mesh,
        in_specs=(P("prow", "pcol"), P("prow", "pcol"), P()),
        out_specs=P("prow", "pcol"),
        check_vma=False,
    )
```

profile of v0, /device:TPU:32, one launch (start us, length us, event | category | flops | bytes accessed | tf_op | source)
XLA Modules:
  0.0 216.6 jit_solution(5361861571704352834)
XLA Ops:
  7.4 0.0 all-reduce.3.cloned.1.call-start
  7.4 1.2 copy.24
  8.6 0.0 copy-start.1
  8.6 0.7 copy-done.1
  9.3 1.0 gather_fusion
  10.3 0.7 slice_select_fusion.1
  11.0 0.8 select_select_fusion
  11.9 0.0 all-reduce.3.cloned.1.call-update
  11.9 0.0 all-gather.2.cloned.1.call-start
  11.9 0.5 all-gather.2.cloned.1.call-update
  12.5 0.7 slice_select_fusion.2
  13.2 128.4 %psum.22 = f32[256,16]{0,1:T(8,128)S(1)} all-reduce(f32[256,16]{0,1:T(8,128)S(1)} %slice_select_fusion.2), channel_id=1, replica_groups=mesh['prow'=32,'pcol'=16] {'prow'}, use_global_device_ids=true, to_apply=%region_2.3 | all-reduce | flops 4096 | bytes 32768 | tf_op jit(solution)/shard_map/psum | solution.py:9
  141.6 34.6 %all_gather.6 = f32[256,256]{0,1:T(8,128)S(1)} all-gather(f32[256,16]{0,1:T(8,128)S(1)} %psum.22), channel_id=1, replica_groups=mesh['prow'=32,'pcol'=16] {'pcol'}, dimensions={1}, use_global_device_ids=true | all-gather | bytes 278528 | tf_op jit(solution)/shard_map/all_gather | solution.py:29
  176.2 0.1 copy.8
  176.4 0.1 convert_add_fusion
  176.5 0.1 triangular_solve.72
  176.6 4.0 %while.2 = (s32[]{:T(128)}, f32[256,256]{1,0:T(8,128)S(1)}, s32[2,2]{1,0:T(2,128)S(1)}, f32[2,128,128]{2,1,0:T(8,128)S(1)}, s32[]{:T(128)}) while((s32[]{:T(128)}, f32[256,256]{1,0:T(8,128)S(1)}, s32[2,2]{1,0:T(2,128)S(1)}, f32[2,128,128]{2,1,0:T(8,128)S(1)}, s32[]{:T(128)}) %tuple.25), condition=%wide.while_cond.1, body=%wide.while_body.1.sunk | while | flops 2 | bytes 131181 | solution.py:13
  176.6 0.6 fusion.14
  177.2 1.3 bitcast_dynamic-update-slice_fusion.2
  178.6 0.6 fusion.14
  179.2 1.3 bitcast_dynamic-update-slice_fusion.2
  180.5 19.7 %custom-call.4 = f32[2,128,128]{1,2,0:T(8,128)S(1)} custom-call(f32[2,128,128]{2,1,0:T(8,128)S(1)} %get-tuple-element.24), custom_call_target="InvertDiagBlocksLowerTriangular" | custom-call | tf_op jit(solution)/shard_map/jit(_solve_triangular)/triangular_solve | solution.py:13
  200.2 0.0 all-reduce.3.cloned.1.call-done
  200.3 0.0 copy-start
  200.3 2.2 %scatter_fusion = f32[1024,256]{1,0:T(8,128)S(1)} fusion(f32[1024,256]{1,0:T(8,128)S(1)} %copy.24, s32[256]{0:T(256)S(1)} %get-tuple-element.37, f32[256,256]{1,0:T(8,128)} %get-tuple-element.33), kind=kCustom, calls=%fused_computation.1 | custom fusion | bytes 787456 | tf_op jit(solution)/shard_map/scatter | solution.py:33
  202.5 0.0 copy-done
  202.5 0.3 fusion.2
  202.8 0.3 convolution_subtract_fusion
  203.1 0.3 fusion.5
  203.4 0.0 all-gather.2.cloned.1.call-done
  203.5 4.0 %fusion = f32[1024,256]{1,0:T(8,128)} fusion(f32[1024,256]{1,0:T(8,128)S(1)} %scatter_fusion, f32[1024,256]{0,1:T(8,128)} %all-gather.2.cloned.1.call-done, f32[128,256]{1,0:T(8,128)S(1)} %fusion.5, f32[128,256]{1,0:T(8,128)S(1)} %fusion.2), kind=kOutput, calls=%fused_computation.5 | convolution fusion | flops 805634048 | bytes 3407872 | tf_op jit(solution)/shard_map/dot_general | solution.py:34
  207.5 1.7 fusion.1
  (8 shorter events, 0.1 us)
Async XLA Ops:
  7.4 192.9 %all-reduce.3.cloned.1.call-start = ((), (), s32[]{:S(2)}) async-start(), calls=%async_computation.1 | async-start | bytes 1048576 | tf_op jit(solution)/shard_map/psum | solution.py:9
  8.6 0.7 copy-start.1
  11.9 191.6 %all-gather.2.cloned.1.call-start = ((), (), s32[]{:S(2)}) async-start(), calls=%async_computation | async-start | bytes 1114112 | tf_op jit(solution)/shard_map/all_gather | solution.py:35
  200.3 2.3 %copy-start = (f32[256,256]{1,0:T(8,128)S(1)}, f32[256,256]{1,0:T(8,128)}, u32[]{:S(2)}) copy-start(f32[256,256]{1,0:T(8,128)} %get-tuple-element.34) | copy-start | bytes 786436
Sparse Core Ops, SparseCore 0:
  12.0 138.7 all-reduce.2
Sparse Core Ops, SparseCore 1:
  14.6 75.2 all-gather.1
where the time goes:
time: 217 us
  blocking collectives  163 us (75%)
  other arithmetic  23.8 us (11%)
  between operations  15 us (7%)
  local copies, waits for them, and re-layouts  9.24 us (4%)
  matrix products  4.89 us (2%)
    psum x1, blocking collectives, broadcast(): return lax.psum(jnp.where(mine, value, jnp.zeros_like(value)), axis)  128 us
    all_gather x1, blocking collectives, local(): diag_block = lax.all_gather(diag_piece, 'pcol', axis=1, tiled=True)  34.6 us
    another operation x4, other arithmetic, solve_block(): jax.scipy.linalg.solve_triangular(diag_block, right_side, lower=True, uni...  19.8 us
  transfers between devices with their start and end apart: 2, of which 0 were waited for; matrix products, arithmetic and copies ran while one was open for 13% of the time, Pallas kernels for 0%

commit v1 on v0

--- a/solution.py
+++ b/solution.py
@@ -26,7 +26,9 @@
         broadcast(slab[:panel_width], "prow", 0),
         broadcast(panel[:panel_width], "prow", 0),
     )
-    diag_block = lax.all_gather(diag_piece, "pcol", axis=1, tiled=True)
+    diag_block = jnp.concatenate(
+        lax.all_to_all(jnp.stack(lax.axis_size("pcol") * [diag_piece]), "pcol", 0, 0), axis=1
+    )
     pivot_rows = lax.psum(masked, "prow")
     upper_rows = solve_block(diag_block, pivot_rows)
     target_row = jnp.where(held_here, local_row, row_count)

time: 217 us -> 331 us (1.53)
  the two profiles are of different devices: /device:TPU:32 before, /device:TPU:1 now
where the time goes in v1:
time: 331 us; the launch traced here: 330 us
  waiting for transfers between devices  137 us (41%)
  blocking collectives  125 us (38%)
  other arithmetic  23.8 us (7%)
  between operations  15 us (5%)
  starting transfers between devices  14.2 us (4%)
  local copies, waits for them, and re-layouts  9.9 us (3%)
  matrix products  4.89 us (1%)
    psum x1, waiting for transfers between devices, broadcast(): return lax.psum(jnp.where(mine, value, jnp.zeros_like(value)), axis)  137 us
    psum x1, blocking collectives, broadcast(): return lax.psum(jnp.where(mine, value, jnp.zeros_like(value)), axis)  125 us
    another operation x4, other arithmetic, solve_block(): jax.scipy.linalg.solve_triangular(diag_block, right_side, lower=True, uni...  19.8 us
    all_to_all x1, starting transfers between devices, local(): lax.all_to_all(jnp.stack(lax.axis_size('pcol') * [diag_piece]), 'pcol', 0...  14.2 us
  transfers between devices with their start and end apart: 3, of which 1 were waited for; matrix products, arithmetic and copies ran while one was open for 9% of the time, Pallas kernels for 0%

profile of v1, /device:TPU:1, one launch (start us, length us, event | category | flops | bytes accessed | tf_op | source)
XLA Modules:
  0.0 330.2 jit_solution(4737349659794616052)
XLA Ops:
  7.4 1.2 copy.22
  8.6 0.7 slice_select_fusion.2
  9.3 125.0 %psum.22 = f32[256,16]{0,1:T(8,128)S(1)} all-reduce(f32[256,16]{0,1:T(8,128)S(1)} %slice_select_fusion.2), channel_id=1, replica_groups=mesh['prow'=32,'pcol'=16] {'prow'}, use_global_device_ids=true, to_apply=%region_2.3 | all-reduce | flops 4096 | bytes 32768 | tf_op jit(solution)/shard_map/psum | solution.py:9
  134.3 0.7 stack.2
  135.0 14.2 %all-to-all-start = ((f32[16,256,16]{1,2,0:T(8,128)}), f32[16,256,16]{1,2,0:T(8,128)S(1)}, u32[]{:S(2)}, u32[]{:S(2)}) async-start(f32[16,256,16]{1,2,0:T(8,128)} %stack.2), calls=%async_computation | async-start | bytes 524288 | tf_op jit(solution)/shard_map/all_to_all | solution.py:30
  149.2 0.0 copy-start.1
  149.2 0.0 all-reduce.3.cloned.1.call-start
  149.2 0.6 copy-done.1
  149.9 0.7 slice_select_fusion.1
  150.6 1.0 gather_fusion
  151.6 0.9 select_select_fusion
  152.5 0.0 all-reduce.3.cloned.1.call-update
  152.5 0.0 all-gather.2.cloned.1.call-start
  152.5 0.5 all-gather.2.cloned.1.call-update
  153.1 136.8 %all-reduce.3.cloned.1.call-done = (f32[256,256]{1,0:T(8,128)}, f32[256,256]{1,0:T(8,128)}) async-done(((f32[256,256]{1,0:T(8,128)}, f32[256,256]{1,0:T(8,128)}), (f32[256,256]{1,0:T(8,128)}, f32[256,256]{1,0:T(8,128)})) %all-reduce.3.cloned.1.call-update) | async-done | bytes 524304 | tf_op jit(solution)/shard_map/psum | solution.py:9
  289.9 2.2 scatter_fusion
  292.1 0.0 all-to-all-done
  292.1 0.1 copy.6
  292.3 0.1 convert_add_fusion
  292.4 0.1 triangular_solve.72
  292.5 4.0 %while.2 = (s32[]{:T(128)}, f32[256,256]{1,0:T(8,128)S(1)}, s32[2,2]{1,0:T(2,128)S(1)}, f32[2,128,128]{2,1,0:T(8,128)S(1)}, s32[]{:T(128)}) while((s32[]{:T(128)}, f32[256,256]{1,0:T(8,128)S(1)}, s32[2,2]{1,0:T(2,128)S(1)}, f32[2,128,128]{2,1,0:T(8,128)S(1)}, s32[]{:T(128)}) %tuple.25), condition=%wide.while_cond.1, body=%wide.while_body.1.sunk | while | flops 2 | bytes 131181 | solution.py:13
  292.5 0.6 fusion.14
  293.1 1.4 bitcast_dynamic-update-slice_fusion.2
  294.5 0.6 fusion.14
  295.0 1.4 bitcast_dynamic-update-slice_fusion.2
  296.4 19.7 %custom-call.4 = f32[2,128,128]{1,2,0:T(8,128)S(1)} custom-call(f32[2,128,128]{2,1,0:T(8,128)S(1)} %get-tuple-element.24), custom_call_target="InvertDiagBlocksLowerTriangular" | custom-call | tf_op jit(solution)/shard_map/jit(_solve_triangular)/triangular_solve | solution.py:13
  316.1 0.3 fusion.2
  316.4 0.3 convolution_subtract_fusion
  316.7 0.3 fusion.5
  317.0 0.0 all-gather.2.cloned.1.call-done
  317.1 4.0 %fusion = f32[1024,256]{1,0:T(8,128)} fusion(f32[1024,256]{1,0:T(8,128)S(1)} %scatter_fusion, f32[1024,256]{0,1:T(8,128)} %all-gather.2.cloned.1.call-done, f32[128,256]{1,0:T(8,128)S(1)} %fusion.5, f32[128,256]{1,0:T(8,128)S(1)} %fusion.2), kind=kOutput, calls=%fused_computation.5 | convolution fusion | flops 805634048 | bytes 3407872 | tf_op jit(solution)/shard_map/dot_general | solution.py:36
  321.1 1.7 fusion.1
  (10 shorter events, 0.1 us)
Async XLA Ops:
  135.0 157.1 %all-to-all-start = ((f32[16,256,16]{1,2,0:T(8,128)}), f32[16,256,16]{1,2,0:T(8,128)S(1)}, u32[]{:S(2)}, u32[]{:S(2)}) async-start(f32[16,256,16]{1,2,0:T(8,128)} %stack.2), calls=%async_computation | async-start | bytes 524288 | tf_op jit(solution)/shard_map/all_to_all | solution.py:30
  149.2 0.7 copy-start.1
  149.2 140.7 %all-reduce.3.cloned.1.call-start = ((), (), s32[]{:S(2)}) async-start(), calls=%async_computation.2 | async-start | bytes 1048576 | tf_op jit(solution)/shard_map/psum | solution.py:9
  152.5 164.6 %all-gather.2.cloned.1.call-start = ((), (), s32[]{:S(2)}) async-start(), calls=%async_computation.1 | async-start | bytes 1114112 | tf_op jit(solution)/shard_map/all_gather | solution.py:37
  292.3 23.8 %copy-start = (f32[256,256]{1,0:T(8,128)S(1)}, f32[256,256]{1,0:T(8,128)}, u32[]{:S(2)}) copy-start(f32[256,256]{1,0:T(8,128)} %get-tuple-element.34) | copy-start | bytes 786436
Sparse Core Ops, SparseCore 0:
  153.2 136.5 all-reduce.2
Sparse Core Ops, SparseCore 1:
  155.2 63.1 all-gather.1
